TPU v7x, 32 devices: a whole 2x2x4 slice. The times are simulated.
32 devices in a mesh: layer: 1, tok: 32 (over z, y, x, core), qry: 1.
Axes of the slice: x: 2, y: 2, z: 4, core: 2. Of those that a mesh axis runs over, the one named last changes fastest.
Arguments:
- train_grads: bfloat16 [128, 32, 28672], P(('layer', 'tok'), None, 'qry'), may hold values from -6 to 6
- train_acts: bfloat16 [128, 32, 8192], P(('layer', 'tok'), None, 'qry'), may hold values from -6 to 6
- token_index: int32 [128, 32], P('tok'), may hold values from 0 to 31, as said below
- query_grads: bfloat16 [64, 4, 28672], P(('layer', 'tok'), None, 'qry'), may hold values from -6 to 6
- query_acts: bfloat16 [64, 4, 8192], P(('layer', 'tok'), None, 'qry'), may hold values from -6 to 6
- out_basis: bfloat16 [256, 28672], P(('layer', 'tok'), 'qry'), may hold values from -0.03125 to 0.03125
- in_basis: bfloat16 [256, 8192], P(('layer', 'tok'), 'qry'), may hold values from -0.0625 to 0.0625
- corrections: bfloat16 [256, 256], P(('layer', 'tok')), may hold values from 0.099609375 to 10
- damp_table: float32 [80], replicated, may hold values from 0.1 to 1
- layer_id: int32 [1], P('layer'), may hold values from 0 to 79
Outputs:
- token_scores: float32 [128, 32, 64], P(('layer', 'tok', 'qry'))
Inputs may be any that keep to these rules, and one draw needn't show every extreme that they name: `token_index`: within one training sequence the 32 indices are distinct.
All inputs are finite; a program needn't handle non-finite values.
Results may differ from a plain program's by a relative error of at most 0.0063.
Values may be sent and summed in bfloat16 or wider, within the bound.
A program may use at most 128 MiB of HBM per device.

v0:
```python
import math

import jax
import jax.numpy as jnp
from jax import lax
from jax.sharding import PartitionSpec as P


def pick_positions(values, token_index):

    def pick_sequence(seq_values, seq_index):
        return jnp.take(seq_values, seq_index, axis=0)

    return jax.vmap(pick_sequence)(values, token_index)


def stack_rows(picked, query_side):
    width = picked.shape[-1]
    return jnp.concatenate([picked.reshape(-1, width), query_side.reshape(-1, width)], axis=0)


def project(row_data, basis_piece):
    return lax.dot_general(
        row_data, basis_piece, (((1,), (1,)), ((), ())), preferred_element_type=jnp.float32
    )


def local(
    train_grads,
    train_acts,
    token_index,
    query_grads,
    query_acts,
    out_basis,
    in_basis,
    corrections,
    damp_table,
    layer_id,
):
    grad_rows = stack_rows(pick_positions(train_grads, token_index), query_grads)
    act_rows = stack_rows(pick_positions(train_acts, token_index), query_acts)
    eigen = corrections.shape[1]
    pieces = (
        lax.all_gather(out_basis, "tok", axis=0, tiled=True),
        lax.all_gather(corrections, "tok", axis=0, tiled=True),
    )
    rot_out = project(grad_rows, pieces[0])
    corr_full = pieces[1]
    rot_in = project(act_rows, lax.all_gather(in_basis, "tok", axis=0, tiled=True))
    rotated = jnp.concatenate([rot_out, rot_in], axis=1)
    seq_count, sel_count = token_index.shape
    query_count, query_len = (query_grads.shape[0], query_grads.shape[1])
    train_part = rotated[: seq_count * sel_count].reshape(seq_count, sel_count, 2 * eigen)
    query_part = rotated[seq_count * sel_count :].reshape(query_count, query_len, 2 * eigen)
    own_count = seq_count // lax.axis_size("qry")
    chosen = (jnp.arange(damp_table.shape[0], dtype=jnp.int32) == layer_id[0]).astype(jnp.float32)
    damping = jnp.sum(damp_table * chosen)
    divisor = corr_full.astype(jnp.float32) + damping
    score_scale = 1.0 / (eigen * math.sqrt(query_len))

    def make_scorer(own_rot):
        token_out = own_rot[:, :, :eigen].reshape(-1, eigen)
        token_in = own_rot[:, :, eigen:].reshape(-1, eigen)
        out_values = token_out.astype(jnp.float32)

        def score_query(query_item):
            rotated_query = lax.dot_general(
                query_item[:, :eigen],
                query_item[:, eigen:],
                (((0,), (0,)), ((), ())),
                preferred_element_type=jnp.float32,
            )
            precond = (rotated_query / divisor).astype(jnp.bfloat16)
            weighted = lax.dot_general(
                token_in, precond, (((1,), (1,)), ((), ())), preferred_element_type=jnp.float32
            )
            return jnp.sum(out_values * weighted, axis=1) * score_scale

        def score_block(pieces, offset):
            values = lax.map(score_query, pieces, batch_size=16)
            return values.T.reshape(own_count, sel_count, pieces.shape[0])

        return score_block

    train_sum, query_sum = lax.psum((train_part, query_part), "qry")
    own_train = lax.dynamic_slice_in_dim(train_sum, lax.axis_index("qry") * own_count, own_count, 0)
    scorer = make_scorer(own_train.astype(jnp.bfloat16))
    token_scores = scorer(
        lax.all_gather(query_sum.astype(jnp.bfloat16), "tok", axis=0, tiled=True), jnp.int32(0)
    )
    return token_scores


def solution(mesh):
    in_specs = (
        P(("layer", "tok"), None, "qry"),
        P(("layer", "tok"), None, "qry"),
        P("tok", None),
        P(("layer", "tok"), None, "qry"),
        P(("layer", "tok"), None, "qry"),
        P(("layer", "tok"), "qry"),
        P(("layer", "tok"), "qry"),
        P(("layer", "tok"), None),
        P(),
        P("layer"),
    )
    out_specs = P(("layer", "tok", "qry"), None, None)
    return jax.shard_map(local, mesh=mesh, in_specs=in_specs, out_specs=out_specs, check_vma=False)
```

profile of v0, /device:TPU:0, one launch (start us, length us, event | category | flops | bytes accessed | tf_op | source)
XLA Modules:
  0.0 247.1 jit_solution(14209762781352969014)
XLA Ops:
  6.5 0.0 copy-start
  6.5 0.0 all-gather.5.cloned.1.call-start
  6.5 0.7 all-gather.5.cloned.1.call-update
  7.3 0.0 all-gather.3.cloned.1.call-start
  7.3 0.7 all-gather.3.cloned.1.call-update
  8.0 0.7 bitcast_or_fusion
  8.7 0.1 reshape.55
  8.8 0.7 compare_and_fusion
  9.5 0.1 broadcast_in_dim.32
  9.6 1.1 reshape.48
  10.7 19.9 %gather_fusion = bf16[128,28672]{1,0:T(8,128)(2,1)} fusion(bf16[4,32,28672]{2,1,0:T(8,128)(2,1)} %param.12, s32[128]{0:T(128)S(1)} %reshape.55), kind=kCustom, calls=%fused_computation | custom fusion | bytes 14681088 | tf_op jit(solution)/shard_map/vmap(jit(_take))/gather | solution.py:12
  30.6 0.0 copy-done
  30.6 0.0 copy-start.1
  30.6 0.0 copy-start.2
  30.6 0.0 copy-start.3
  30.6 8.2 %gather_fusion.1 = bf16[128,8192]{1,0:T(8,128)(2,1)} fusion(bf16[4,32,8192]{2,1,0:T(8,128)(2,1)S(1)} %copy-done, s32[128]{0:T(128)S(1)} %reshape.55), kind=kCustom, calls=%fused_computation.1 | custom fusion | bytes 4195328 | tf_op jit(solution)/shard_map/vmap(jit(_take))/gather | solution.py:12
  38.8 0.0 copy-done.1
  39.5 0.0 copy-done.2
  39.5 44.1 %all_gather.15 = bf16[256,256]{1,0:T(8,128)(2,1)S(1)} all-gather(bf16[8,256]{1,0:T(8,128)(2,1)S(1)} %copy-done.2), channel_id=1, replica_groups=mesh['layer'=1,'tok'=32,'qry'=1] {'tok'}, dimensions={0}, use_global_device_ids=true | all-gather | bytes 135168 | tf_op jit(solution)/shard_map/all_gather | solution.py:45
  83.6 0.0 copy-done.3
  83.6 0.7 fusion.15
  84.3 0.7 convert_add_fusion
  85.0 3.3 %broadcast_select_fusion.1 = bf16[128,8192]{1,0:T(8,128)(2,1)} fusion(bf16[128,8192]{1,0:T(8,128)(2,1)} %gather_fusion.1, pred[128]{0:T(512)(128)(4,1)S(1)} %broadcast_in_dim.32), kind=kLoop, calls=%fused_computation.20 | loop fusion | flops 1048576 | bytes 4194432 | tf_op jit(solution)/shard_map/vmap(jit(_take))/select_n | solution.py:12
  88.3 6.8 %broadcast_select_fusion = bf16[128,28672]{1,0:T(8,128)(2,1)} fusion(bf16[128,28672]{1,0:T(8,128)(2,1)} %gather_fusion, pred[128]{0:T(512)(128)(4,1)S(1)} %broadcast_in_dim.32), kind=kLoop, calls=%fused_computation.15 | loop fusion | flops 3670016 | bytes 14680192 | tf_op jit(solution)/shard_map/vmap(jit(_take))/select_n | solution.py:12
  95.1 0.0 all-gather.5.cloned.1.call-done
  95.1 4.4 %fusion.11 = bf16[136,256]{1,0:T(8,128)(2,1)S(1)} fusion(bf16[256,8192]{1,0:T(8,128)(2,1)} %all-gather.5.cloned.1.call-done, bf16[8,8192]{1,0:T(8,128)(2,1)S(1)} %reshape.49, bf16[128,8192]{1,0:T(8,128)(2,1)} %broadcast_select_fusion.1), kind=kOutput, calls=%fused_computation.16 | convolution fusion | flops 574881792 | bytes 6492160 | tf_op jit(solution)/shard_map/dot_general | solution.py:23
  99.5 82.6 %all-gather.3.cloned.1.call-done = bf16[256,28672]{1,0:T(8,128)(2,1)} async-done(((bf16[8,28672]{1,0:T(8,128)(2,1)}), bf16[256,28672]{1,0:T(8,128)(2,1)}) %all-gather.3.cloned.1.call-update) | async-done | bytes 14680080 | tf_op jit(solution)/shard_map/all_gather | solution.py:44
  182.0 12.4 %fusion.7 = bf16[136,256]{1,0:T(8,128)(2,1)S(1)} fusion(bf16[256,28672]{1,0:T(8,128)(2,1)} %all-gather.3.cloned.1.call-done, bf16[8,28672]{1,0:T(8,128)(2,1)S(1)} %reshape.48, bf16[128,28672]{1,0:T(8,128)(2,1)} %broadcast_select_fusion), kind=kOutput, calls=%fused_computation.11 | convolution fusion | flops 2012086272 | bytes 22548480 | tf_op jit(solution)/shard_map/dot_general | solution.py:23
  194.5 0.1 copy.15
  194.6 39.3 %all_gather.14 = bf16[64,4,512]{2,1,0:T(4,128)(2,1)S(1)} all-gather(bf16[2,4,512]{2,1,0:T(4,128)(2,1)S(1)} %convert_element_type.24), channel_id=1, replica_groups=mesh['layer'=1,'tok'=32,'qry'=1] {'tok'}, dimensions={0}, use_global_device_ids=true | all-gather | bytes 270336 | tf_op jit(solution)/shard_map/all_gather | solution.py:89
  233.9 5.6 %while.10 = (s32[]{:T(128)}, f32[4,16,128]{2,1,0:T(8,128)S(1)}, f32[128,256]{0,1:T(8,128)S(1)}, bf16[4,16,4,512]{3,2,1,0:T(4,128)(2,1)S(1)}, f32[256,256]{1,0:T(...) while((s32[]{:T(128)}, f32[4,16,128]{2,1,0:T(8,128)S(1)}, f32[128,256]{0,1:T(8,128)S(1)}, ...), condition=%wide.region_3.4_spmd, body=%wide.region_1.3_spmd.sunk | while | flops 279969792 | bytes 680021 | solution.py:80
  234.0 1.3 fusion.28
  235.4 1.3 fusion.28
  236.8 1.3 fusion.28
  238.2 1.3 fusion.28
  239.5 0.7 copy.16
  (16 shorter events, 0.3 us)
Async XLA Ops:
  6.5 24.0 %copy-start = (bf16[4,32,8192]{2,1,0:T(8,128)(2,1)S(1)}, bf16[4,32,8192]{2,1,0:T(8,128)(2,1)}, u32[]{:S(2)}) copy-start(bf16[4,32,8192]{2,1,0:T(8,128)(2,1)} %param.13) | copy-start | bytes 6291460
  6.5 88.5 %all-gather.5.cloned.1.call-start = ((), (), s32[]{:S(2)}) async-start(), calls=%async_computation.1 | async-start | bytes 4325376 | tf_op jit(solution)/shard_map/all_gather | solution.py:49
  7.3 174.8 %all-gather.3.cloned.1.call-start = ((), (), s32[]{:S(2)}) async-start(), calls=%async_computation | async-start | bytes 15138816 | tf_op jit(solution)/shard_map/all_gather | solution.py:44
  30.6 8.2 %copy-start.1 = (bf16[2,4,8192]{2,1,0:T(4,128)(2,1)S(1)}, bf16[2,4,8192]{2,1,0:T(4,128)(2,1)}, u32[]{:S(2)}) copy-start(bf16[2,4,8192]{2,1,0:T(4,128)(2,1)} %param.16) | copy-start | bytes 393220
  30.6 8.9 %copy-start.2 = (bf16[8,256]{1,0:T(8,128)(2,1)S(1)}, bf16[8,256]{1,0:T(8,128)(2,1)}, u32[]{:S(2)}) copy-start(bf16[8,256]{1,0:T(8,128)(2,1)} %param.19) | copy-start | bytes 12292
  30.6 53.0 %copy-start.3 = (f32[80]{0:T(128)S(1)}, f32[80]{0:T(128)}, u32[]{:S(2)}) copy-start(f32[80]{0:T(128)} %param.20) | copy-start | bytes 964
Sparse Core Ops, SparseCore 0:
  10.2 64.9 all-gather.4
  78.0 103.9 all-gather.2
where the time goes:
time: 247 us
  waiting for transfers between devices  84 us (34%)
  blocking collectives  83.4 us (34%)
  local copies, waits for them, and re-layouts  30.4 us (12%)
  matrix products  22 us (9%)
  between operations  14.2 us (6%)
  other arithmetic  12.9 us (5%)
    all_gather x1, waiting for transfers between devices, local(): lax.all_gather(out_basis, 'tok', axis=0, tiled=True)  82.6 us
    all_gather x1, blocking collectives, local(): lax.all_gather(corrections, 'tok', axis=0, tiled=True)  44.1 us
    all_gather x1, blocking collectives, local(): lax.all_gather(query_sum.astype(jnp.bfloat16), 'tok', axis=0, tiled=True)  39.3 us
    gather x3, local copies, waits for them, and re-layouts, pick_sequence(): return jnp.take(seq_values, seq_index, axis=0)  28.2 us
    dot_general x2, matrix products, project(): lax.dot_general(row_data, basis_piece, (((1,), (1,)), ((), ())), preferre...  16.7 us
    select_n x2, other arithmetic, pick_sequence(): return jnp.take(seq_values, seq_index, axis=0)  10.1 us
    dot_general x4, matrix products, score_query(): lax.dot_general(token_in, precond, (((1,), (1,)), ((), ())), preferred_el...  5.28 us
  transfers between devices with their start and end apart: 2, of which 1 were waited for; matrix products, arithmetic and copies ran while one was open for 19% of the time, Pallas kernels for 0%

commit v1 on v0

v1 whole, which is shorter than its diff:
```python
import math

import jax
import jax.numpy as jnp
from jax import lax
from jax.experimental import pallas as pl
from jax.experimental.pallas import tpu as pltpu
from jax.sharding import PartitionSpec as P

AXES = ("layer", "tok", "qry")
CHIPS = (4, 2, 2)
KINDS = ("zxy",) * 5 + ("yzx",) * 3 + ("xyz",)


def pick_positions(values, token_index):

    def pick_sequence(seq_values, seq_index):
        return jnp.take(seq_values, seq_index, axis=0)

    return jax.vmap(pick_sequence)(values, token_index)


def stack_rows(picked, query_side):
    width = picked.shape[-1]
    return jnp.concatenate([picked.reshape(-1, width), query_side.reshape(-1, width)], axis=0)


def project(row_data, basis_piece):
    return lax.dot_general(
        row_data, basis_piece, (((1,), (1,)), ((), ())), preferred_element_type=jnp.float32
    )


def make_scorer(own_rot, divisor, eigen, query_len, own_count, sel_count):
    score_scale = 1.0 / (eigen * math.sqrt(query_len))
    token_out = own_rot[:, :, :eigen].reshape(-1, eigen)
    token_in = own_rot[:, :, eigen:].reshape(-1, eigen)
    out_values = token_out.astype(jnp.float32)

    def score_query(query_item):
        rotated_query = lax.dot_general(
            query_item[:, :eigen],
            query_item[:, eigen:],
            (((0,), (0,)), ((), ())),
            preferred_element_type=jnp.float32,
        )
        precond = (rotated_query / divisor).astype(jnp.bfloat16)
        weighted = lax.dot_general(
            token_in, precond, (((1,), (1,)), ((), ())), preferred_element_type=jnp.float32
        )
        return jnp.sum(out_values * weighted, axis=1) * score_scale

    def score_block(pieces):
        values = lax.map(score_query, pieces, batch_size=16)
        return values.T.reshape(own_count, sel_count, pieces.shape[0])

    return score_block


def pick_damping(damp_table, layer_id):
    chosen = (jnp.arange(damp_table.shape[0], dtype=jnp.int32) == layer_id[0]).astype(jnp.float32)
    return jnp.sum(damp_table * chosen)


def local(
    train_grads,
    train_acts,
    token_index,
    query_grads,
    query_acts,
    out_basis,
    in_basis,
    corrections,
    damp_table,
    layer_id,
):
    grad_rows = stack_rows(pick_positions(train_grads, token_index), query_grads)
    act_rows = stack_rows(pick_positions(train_acts, token_index), query_acts)
    eigen = corrections.shape[1]
    pieces = (
        lax.all_gather(out_basis, "tok", axis=0, tiled=True),
        lax.all_gather(corrections, "tok", axis=0, tiled=True),
    )
    rot_out = project(grad_rows, pieces[0])
    corr_full = pieces[1]
    rot_in = project(act_rows, lax.all_gather(in_basis, "tok", axis=0, tiled=True))
    rotated = jnp.concatenate([rot_out, rot_in], axis=1)
    seq_count, sel_count = token_index.shape
    query_count, query_len = (query_grads.shape[0], query_grads.shape[1])
    train_part = rotated[: seq_count * sel_count].reshape(seq_count, sel_count, 2 * eigen)
    query_part = rotated[seq_count * sel_count :].reshape(query_count, query_len, 2 * eigen)
    own_count = seq_count // lax.axis_size("qry")
    divisor = corr_full.astype(jnp.float32) + pick_damping(damp_table, layer_id)
    train_sum, query_sum = lax.psum((train_part, query_part), "qry")
    own_train = lax.dynamic_slice_in_dim(train_sum, lax.axis_index("qry") * own_count, own_count, 0)
    scorer = make_scorer(
        own_train.astype(jnp.bfloat16), divisor, eigen, query_len, own_count, sel_count
    )
    return scorer(lax.all_gather(query_sum.astype(jnp.bfloat16), "tok", axis=0, tiled=True))


def rotate_kernel(
    stack_ref,
    grads_ref,
    acts_ref,
    rot_ref,
    query_ref,
    corr_ref,
    basis,
    rows,
    partner,
    acc,
    part_out,
    part_in,
    qpart_out,
    qpart_in,
    queries,
    own_sem,
    pair_send,
    pair_recv,
    up_send,
    down_send,
    z_recv,
    side_send,
    side_recv,
    query_send,
    query_recv,
):
    me = lax.axis_index("tok")
    core = lax.rem(me, 2)
    chip = me // 2
    x = lax.rem(me // 2, 2)
    y = lax.rem(me // 4, 2)
    z = me // 8
    nz = CHIPS[0]
    count = 2 * nz * CHIPS[1] * CHIPS[2]
    sibling = me + 1 - 2 * core
    x_peer = me + 2 - 4 * x
    y_peer = me + 4 - 8 * y
    train, wide_out = grads_ref.shape
    half_out = wide_out // 2
    half_in = acts_ref.shape[1] // 2
    eigen = corr_ref.shape[1]
    chunk = (half_out + half_in) // len(KINDS)
    out_chunks = half_out // chunk

    def span(j):
        extra = eigen if j == len(KINDS) - 1 else 0
        return pl.ds(j * chunk, chunk + extra)

    def remote(src, dst, send, recv, device):
        return pltpu.make_async_remote_copy(
            src_ref=src,
            dst_ref=dst,
            send_sem=send,
            recv_sem=recv,
            device_id=(0, device, 0),
            device_id_type=pl.DeviceIdType.MESH,
        )

    own_copies = [
        pltpu.make_async_copy(
            grads_ref.at[:, pl.ds(core * half_out, half_out)],
            rows.at[pl.ds(0, train), pl.ds(0, half_out)],
            own_sem.at[0],
        ),
        pltpu.make_async_copy(
            acts_ref.at[:, pl.ds(core * half_in, half_in)],
            rows.at[pl.ds(0, train), pl.ds(half_out, half_in)],
            own_sem.at[1],
        ),
    ]
    for copy in own_copies:
        copy.start()

    barrier = pltpu.get_barrier_semaphore()

    def greet(s, carry):
        pl.semaphore_signal(
            barrier,
            inc=1,
            device_id=(0, lax.rem(me + s, count), 0),
            device_id_type=pl.DeviceIdType.MESH,
        )
        return carry

    lax.fori_loop(1, count, greet, 0)
    pl.semaphore_wait(barrier, count - 1)

    stack_copy = remote(stack_ref.at[1 - core], partner, pair_send.at[0], pair_recv.at[0], sibling)
    stack_copy.start()
    row_copies = [
        remote(
            grads_ref.at[:, pl.ds((1 - core) * half_out, half_out)],
            rows.at[pl.ds(train, train), pl.ds(0, half_out)],
            pair_send.at[1],
            pair_recv.at[1],
            sibling,
        ),
        remote(
            acts_ref.at[:, pl.ds((1 - core) * half_in, half_in)],
            rows.at[pl.ds(train, train), pl.ds(half_out, half_in)],
            pair_send.at[2],
            pair_recv.at[2],
            sibling,
        ),
    ]
    for copy in row_copies:
        copy.start()
    acc[...] = jnp.zeros_like(acc)
    stack_copy.wait_recv()

    def build(j):
        cols = span(j)
        own = stack_ref[core, :, cols].astype(jnp.float32)
        other = partner[:, cols].astype(jnp.float32)
        first = jnp.where(core == 0, own, other)
        second = jnp.where(core == 0, other, own)
        basis[y, x, z, :, cols] = jnp.concatenate([first[:8], second[:8]], axis=0).astype(
            jnp.bfloat16
        )
        rows[pl.ds(2 * train, 16), cols] = jnp.concatenate(
            [first[8:], second[8:]], axis=0
        ).astype(jnp.bfloat16)

    def z_block(j, source):
        cols = span(j)
        if KINDS[j] == "zxy":
            return basis.at[y, x, source, :, cols]
        if KINDS[j] == "yzx":
            return basis.at[:, x, source, :, cols]
        return basis.at[:, :, source, :, cols]

    def x_block(j, at_x):
        cols = span(j)
        if KINDS[j] == "zxy":
            return basis.at[y, at_x, :, :, cols]
        if KINDS[j] == "yzx":
            return basis.at[:, at_x, :, :, cols]
        return basis.at[y, at_x, z, :, cols]

    def y_block(j, at_y):
        cols = span(j)
        if KINDS[j] == "zxy":
            return basis.at[at_y, :, :, :, cols]
        if KINDS[j] == "yzx":
            return basis.at[at_y, x, z, :, cols]
        return basis.at[at_y, :, z, :, cols]

    def up_copy(j, source):
        ref = z_block(j, source)
        return remote(ref, ref, up_send.at[j, source], z_recv.at[j, source], me + 8)

    def down_copy(j, source):
        ref = z_block(j, source)
        return remote(ref, ref, down_send.at[j, source], z_recv.at[j, source], me - 8)

    def x_copy(j, at_x):
        ref = x_block(j, at_x)
        return remote(ref, ref, side_send.at[0, j], side_recv.at[0, j], x_peer)

    def y_copy(j, at_y):
        ref = y_block(j, at_y)
        return remote(ref, ref, side_send.at[1, j], side_recv.at[1, j], y_peer)

    def z_start(j):
        @pl.when(z < nz - 1)
        def _():
            up_copy(j, z).start()

        @pl.when(z > 0)
        def _():
            down_copy(j, z).start()

    def z_step(j, s):
        @pl.when(z - s >= 0)
        def _():
            up_copy(j, z - s).wait_recv()

            @pl.when(z < nz - 1)
            def _():
                up_copy(j, z - s).start()

        @pl.when(z + s < nz)
        def _():
            down_copy(j, z + s).wait_recv()

            @pl.when(z > 0)
            def _():
                down_copy(j, z + s).start()

    def x_start(j):
        x_copy(j, x).start()

    def y_start(j):
        y_copy(j, y).start()

    def x_wait(j):
        x_copy(j, 1 - x).wait_recv()

    def y_wait(j):
        y_copy(j, 1 - y).wait_recv()

    def natural(cols):
        return jnp.concatenate(
            [
                basis[b, a, c, :, cols]
                for c in range(nz)
                for b in range(CHIPS[1])
                for a in range(CHIPS[2])
            ],
            axis=0,
        )

    def compute(j):
        side = 0 if j < out_chunks else 1
        cols = pl.ds(j * chunk, chunk)
        acc[side] += lax.dot_general(
            rows[:, cols],
            natural(cols),
            (((1,), (1,)), ((), ())),
            preferred_element_type=jnp.float32,
        )

    last = len(KINDS) - 1
    for j in (0, 5, 8, 1, 6, 2, 7, 3, 4):
        build(j)
        {"z": z_start, "x": x_start, "y": y_start}[KINDS[j][0]](j)
    for j in (0, 1, 2):
        z_step(j, 1)
    x_wait(8)
    y_start(8)
    for j in (0, 1, 2):
        z_step(j, 2)
    for j in (0, 1, 2):
        z_step(j, 3)
        x_start(j)
    y_wait(5)
    z_start(5)
    z_step(3, 1)
    z_step(4, 1)
    x_wait(0)
    y_start(0)
    z_step(5, 1)
    z_step(3, 2)
    z_step(4, 2)
    y_wait(6)
    z_start(6)
    x_wait(1)
    y_start(1)
    z_step(5, 2)
    z_step(3, 3)
    x_start(3)
    x_wait(2)
    y_start(2)
    z_step(5, 3)
    x_start(5)
    z_step(4, 3)
    x_start(4)
    z_step(6, 1)
    y_wait(7)
    z_start(7)
    for copy in own_copies:
        copy.wait()
    for copy in row_copies:
        copy.wait_recv()
    y_wait(0)
    compute(0)
    z_step(6, 2)
    x_wait(3)
    y_start(3)
    z_step(6, 3)
    x_start(6)
    y_wait(8)
    z_start(8)
    z_step(7, 1)
    x_wait(4)
    y_start(4)
    y_wait(1)
    compute(1)
    z_step(7, 2)
    x_wait(5)
    compute(5)
    z_step(8, 1)
    z_step(7, 3)
    x_start(7)
    y_wait(2)
    compute(2)
    z_step(8, 2)
    y_wait(3)
    compute(3)
    x_wait(6)
    compute(6)
    z_step(8, 3)
    compute(8)
    y_wait(4)
    compute(4)
    x_wait(7)
    compute(7)

    qpart_out[...] = acc[1 - core, pl.ds(2 * train, 16), :]
    qpart_copy = remote(qpart_out, qpart_in, pair_send.at[3], pair_recv.at[3], sibling)
    qpart_copy.start()
    part_out[...] = acc[:, pl.ds(train, train), :]
    part_copy = remote(part_out, part_in, pair_send.at[4], pair_recv.at[4], sibling)
    part_copy.start()
    qpart_copy.wait_recv()
    queries[core, chip] = (acc[core, pl.ds(2 * train, 16), :] + qpart_in[...]).astype(jnp.bfloat16)

    def query_copy(source, target):
        ref = queries.at[lax.rem(source, 2), source // 2]
        return remote(ref, ref, query_send.at[target], query_recv.at[source], target)

    def send_query(s, carry):
        query_copy(me, lax.rem(me + s, count)).start()
        return carry

    lax.fori_loop(1, count, send_query, 0)
    corr_ref[...] = natural(pl.ds(half_out + half_in, eigen))
    part_copy.wait_recv()
    rot_ref[...] = (acc[:, pl.ds(0, train), :] + part_in[...]).astype(jnp.bfloat16)

    def wait_query(s, carry):
        source = lax.rem(me + s, count)
        query_copy(source, source).wait_recv()
        return carry

    lax.fori_loop(1, count, wait_query, 0)
    query_ref[...] = queries[...].reshape(query_ref.shape)

    stack_copy.wait_send()
    for copy in row_copies:
        copy.wait_send()
    qpart_copy.wait_send()
    part_copy.wait_send()
    for j in range(last + 1):
        x_copy(j, x).wait_send()
        y_copy(j, y).wait_send()
        for s in range(nz):

            @pl.when(jnp.logical_and(z < nz - 1, z - s >= 0))
            def _():
                up_copy(j, z - s).wait_send()

            @pl.when(jnp.logical_and(z > 0, z + s < nz))
            def _():
                down_copy(j, z + s).wait_send()

    def finish_query(s, carry):
        query_copy(me, lax.rem(me + s, count)).wait_send()
        return carry

    lax.fori_loop(1, count, finish_query, 0)


def rotate_all(stack, grads, acts, eigen):
    train, wide = grads.shape
    total = stack.shape[2]
    nz, ny, nx = CHIPS
    chips = nz * ny * nx
    n = len(KINDS)
    dma = pltpu.SemaphoreType.DMA
    vmem = pl.BlockSpec(memory_space=pltpu.VMEM)
    hbm = pl.BlockSpec(memory_space=pl.ANY)
    return pl.pallas_call(
        rotate_kernel,
        out_shape=(
            jax.ShapeDtypeStruct((2, train, eigen), jnp.bfloat16),
            jax.ShapeDtypeStruct((2, chips * 16, eigen), jnp.bfloat16),
            jax.ShapeDtypeStruct((eigen, eigen), jnp.bfloat16),
        ),
        in_specs=[vmem, hbm, hbm],
        out_specs=(vmem, vmem, vmem),
        scratch_shapes=[
            pltpu.VMEM((ny, nx, nz, 16, total), jnp.bfloat16),
            pltpu.VMEM((2 * train + 16, total), jnp.bfloat16),
            pltpu.VMEM((16, total), jnp.bfloat16),
            pltpu.VMEM((2, 2 * train + 16, eigen), jnp.float32),
            pltpu.VMEM((2, train, eigen), jnp.float32),
            pltpu.VMEM((2, train, eigen), jnp.float32),
            pltpu.VMEM((16, eigen), jnp.float32),
            pltpu.VMEM((16, eigen), jnp.float32),
            pltpu.VMEM((2, chips, 16, eigen), jnp.bfloat16),
            dma((2,)),
            dma((5,)),
            dma((5,)),
            dma((n, nz)),
            dma((n, nz)),
            dma((n, nz)),
            dma((2, n)),
            dma((2, n)),
            dma((2 * chips,)),
            dma((2 * chips,)),
        ],
        compiler_params=pltpu.CompilerParams(
            collective_id=0, has_side_effects=True, vmem_limit_bytes=44 * 1024 * 1024
        ),
        cost_estimate=pl.CostEstimate(
            flops=4 * train * total * eigen, bytes_accessed=4 * train * wide, transcendentals=0
        ),
    )(stack, grads, acts)


def local_fused(
    train_grads,
    train_acts,
    token_index,
    query_grads,
    query_acts,
    out_basis,
    in_basis,
    corrections,
    damp_table,
    layer_id,
):
    eigen = corrections.shape[1]
    seq_count, sel_count = token_index.shape
    length = train_grads.shape[1]
    query_count, query_len = query_grads.shape[:2]
    rows_q = query_count * query_len
    wide_out, wide_in = out_basis.shape[1], in_basis.shape[1]
    out_rows = jnp.concatenate([out_basis, query_grads.reshape(rows_q, wide_out)], axis=0)
    in_rows = jnp.concatenate([in_basis, query_acts.reshape(rows_q, wide_in)], axis=0)
    corr_rows = jnp.concatenate([corrections, jnp.zeros((rows_q, eigen), corrections.dtype)], axis=0)
    stack = jnp.stack(
        [
            jnp.concatenate(
                [
                    out_rows[:, h * (wide_out // 2) : (h + 1) * (wide_out // 2)],
                    in_rows[:, h * (wide_in // 2) : (h + 1) * (wide_in // 2)],
                    corr_rows,
                ],
                axis=1,
            )
            for h in range(2)
        ],
        axis=0,
    )
    rot, queries, corr = rotate_all(
        stack,
        train_grads.reshape(-1, wide_out),
        train_acts.reshape(-1, wide_in),
        eigen,
    )
    one_hot = (token_index[:, :, None] == jnp.arange(length, dtype=token_index.dtype)).astype(
        jnp.bfloat16
    )
    positions = jnp.concatenate([rot[0], rot[1]], axis=1).reshape(seq_count, length, 2 * eigen)
    own_rot = jnp.einsum(
        "sjl,sle->sje", one_hot, positions, preferred_element_type=jnp.float32
    ).astype(jnp.bfloat16)
    divisor = corr.astype(jnp.float32) + pick_damping(damp_table, layer_id)
    scorer = make_scorer(own_rot, divisor, eigen, query_len, seq_count, sel_count)
    pieces = jnp.concatenate([queries[0], queries[1]], axis=1)
    return scorer(pieces.reshape(-1, query_len, 2 * eigen))


def solution(mesh):
    in_specs = (
        P(("layer", "tok"), None, "qry"),
        P(("layer", "tok"), None, "qry"),
        P("tok", None),
        P(("layer", "tok"), None, "qry"),
        P(("layer", "tok"), None, "qry"),
        P(("layer", "tok"), "qry"),
        P(("layer", "tok"), "qry"),
        P(("layer", "tok"), None),
        P(),
        P("layer"),
    )
    out_specs = P(("layer", "tok", "qry"), None, None)
    sizes = tuple(mesh.shape[axis] for axis in AXES)
    fused = sizes == (1, 2 * CHIPS[0] * CHIPS[1] * CHIPS[2], 1)
    return jax.shard_map(
        local_fused if fused else local,
        mesh=mesh,
        in_specs=in_specs,
        out_specs=out_specs,
        check_vma=False,
    )
```

time: 247 us -> 111 us (0.45)
  Pallas kernels: 0 us -> 96.9 us
  waiting for transfers between devices: 84 us -> 0 us
  blocking collectives: 83.4 us -> 0 us
  local copies, waits for them, and re-layouts: 30.4 us -> 4.81 us
  matrix products: 22 us -> 5.46 us
  between operations: 14.2 us -> 0.87 us
  other arithmetic: 12.9 us -> 1.66 us
    pallas_call x0 -> x1, Pallas kernels: none -> 96.9 us  [rotate_all(): pl.pallas_call(rotate_kernel, out_shape=(jax.ShapeDtypeStruct((2, train,...]
    all_gather x2 -> x0, blocking collectives: 83.4 us -> none  [the longest x1 44.1 us: local(): lax.all_gather(corrections, 'tok', axis=0, tiled=True)]
    all_gather x2 -> x0, waiting for transfers between devices: 82.6 us -> none  [the longest x1 82.6 us: local(): lax.all_gather(out_basis, 'tok', axis=0, tiled=True)]
    gather x3 -> x0, local copies, waits for them, and re-layouts: 28.2 us -> none  [pick_sequence(): return jnp.take(seq_values, seq_index, axis=0)]
    dot_general x2 -> x1, matrix products: 16.7 us -> 0.22 us  [local_fused(): jnp.einsum('sjl,sle->sje', one_hot, positions, preferred_element_type=jnp...]
    select_n x2 -> x0, other arithmetic: 10.1 us -> none  [pick_sequence(): return jnp.take(seq_values, seq_index, axis=0)]
    unnamed x8 -> x16, local copies, waits for them, and re-layouts: 0.02 us -> 3.48 us
  transfers between devices with their start and end apart: 2 -> 0, of which waited for: 1 -> 0; matrix products, arithmetic and copies ran while one was open for 19% -> 0% of each run, Pallas kernels for 0% -> 0%
where the time goes in v1:
time: 111 us; the launch traced here: 110 us
  Pallas kernels  96.9 us (87%)
  matrix products  5.46 us (5%)
  local copies, waits for them, and re-layouts  4.81 us (4%)
  other arithmetic  1.66 us (1%)
    pallas_call x1, Pallas kernels, rotate_all(): pl.pallas_call(rotate_kernel, out_shape=(jax.ShapeDtypeStruct((2, train,...  96.9 us
    dot_general x4, matrix products, score_query(): lax.dot_general(token_in, precond, (((1,), (1,)), ((), ())), preferred_el...  5.23 us
    unnamed x16, local copies, waits for them, and re-layouts  3.48 us

profile of v1, /device:TPU:0, one launch (start us, length us, event | category | flops | bytes accessed | tf_op | source)
XLA Modules:
  0.0 109.9 jit_solution(1261572433179040631)
XLA Ops:
  0.0 0.0 copy-start.1
  0.0 1.1 %constant_dynamic-update-slice_fusion.1 = bf16[16,28672]{1,0:T(8,128)(2,1)S(1)} fusion(bf16[8,28672]{1,0:T(8,128)(2,1)} %param.17), kind=kLoop, calls=%fused_computation.26 | loop fusion | bytes 917504
  1.1 0.0 copy-done.1
  1.2 0.1 reshape.45
  1.3 0.0 copy-start.2
  1.3 0.0 copy-start.3
  1.3 0.0 copy-start.4
  1.4 0.1 fusion.18
  1.4 0.8 copy-done.2
  2.2 0.1 copy-done.3
  2.4 0.0 copy-done.4
  2.4 0.1 fusion.11
  2.5 0.0 copy-start
  2.5 0.1 pad_maximum_fusion.stack_ref
  2.6 1.5 %copy-done = bf16[4,32,8192]{2,1,0:T(8,128)(2,1)S(1)} copy-done((bf16[4,32,8192]{2,1,0:T(8,128)(2,1)S(1)}, bf16[4,32,8192]{2,1,0:T(8,128)(2,1)}, u32[]{:S(2)}) %copy-start) | copy-done | bytes 2097176
  4.0 0.0 copy-start.5
  4.0 96.9 %shard_map.100 = (bf16[2,128,256]{2,1,0:T(8,128)(2,1)S(1)}, bf16[2,256,256]{2,1,0:T(8,128)(2,1)S(1)}, bf16[256,256]{1,0:T(8,128)(2,1)S(1)}) custom-call(bf16[2,16,18688]{2,1,0:T(8,128)(2,1)S(1)} %pad_maximum_fusion.stack_ref, bf16[128,28672]{1,0:T(8,128)(2,1)} %bitcast.38, bf16[128,8192]{1,0:T(8,128)(2,1)S(1)} %bitcast.37), custom_call_target="tpu_custom_call" | custom-call | flops 2449473536 | bytes 14680064 | tf_op jit(solution)/shard_map/pallas_call | solution.py:465
  101.0 0.0 copy-done.5
  101.0 0.2 convolution_convert_fusion
  101.2 0.0 copy-start.6
  101.3 0.1 copy.11
  101.5 0.1 pad_maximum_fusion.1
  102.3 0.0 copy-done.6
  102.3 0.7 fusion.16
  102.9 0.6 convert_add_fusion
  103.6 5.5 %while.10 = (s32[]{:T(128)}, f32[4,16,128]{2,1,0:T(8,128)S(1)}, f32[128,256]{0,1:T(8,128)S(1)}, bf16[4,16,4,512]{3,2,1,0:T(4,128)(2,1)S(1)}, f32[256,256]{1,0:T(...) while((s32[]{:T(128)}, f32[4,16,128]{2,1,0:T(8,128)S(1)}, f32[128,256]{0,1:T(8,128)S(1)}, ...), condition=%wide.region_3.4_spmd, body=%wide.region_1.3_spmd.sunk | while | flops 279969792 | bytes 680021 | solution.py:54
  103.6 1.3 %fusion.30 = f32[16,128]{1,0:T(8,128)S(1)} fusion(f32[128,256]{0,1:T(8,128)S(1)} %get-tuple-element.127, f32[256,256]{1,0:T(8,128)S(1)} %get-tuple-element.129, bf16[128,256]{1,0:T(8,128)(2,1)S(1)} %get-tuple-element.130, bf16[16,4,512]{2,1,0:T(4,128)(2,1)S(1)} %dynamic-slice_bitcast_fusion.2), kind=kOutput, calls=%fused_computation.2.clone.1 | convolution fusion | flops 279967744 | bytes 532480 | tf_op jit(solution)/shard_map/while/body/eval_jaxpr/vmap()/dot_general | solution.py:48
  105.0 1.3 %fusion.30 = f32[16,128]{1,0:T(8,128)S(1)} fusion(f32[128,256]{0,1:T(8,128)S(1)} %get-tuple-element.127, f32[256,256]{1,0:T(8,128)S(1)} %get-tuple-element.129, bf16[128,256]{1,0:T(8,128)(2,1)S(1)} %get-tuple-element.130, bf16[16,4,512]{2,1,0:T(4,128)(2,1)S(1)} %dynamic-slice_bitcast_fusion.2), kind=kOutput, calls=%fused_computation.2.clone.1 | convolution fusion | flops 279967744 | bytes 532480 | tf_op jit(solution)/shard_map/while/body/eval_jaxpr/vmap()/dot_general | solution.py:48
  106.4 1.3 %fusion.30 = f32[16,128]{1,0:T(8,128)S(1)} fusion(f32[128,256]{0,1:T(8,128)S(1)} %get-tuple-element.127, f32[256,256]{1,0:T(8,128)S(1)} %get-tuple-element.129, bf16[128,256]{1,0:T(8,128)(2,1)S(1)} %get-tuple-element.130, bf16[16,4,512]{2,1,0:T(4,128)(2,1)S(1)} %dynamic-slice_bitcast_fusion.2), kind=kOutput, calls=%fused_computation.2.clone.1 | convolution fusion | flops 279967744 | bytes 532480 | tf_op jit(solution)/shard_map/while/body/eval_jaxpr/vmap()/dot_general | solution.py:48
  107.8 1.3 %fusion.30 = f32[16,128]{1,0:T(8,128)S(1)} fusion(f32[128,256]{0,1:T(8,128)S(1)} %get-tuple-element.127, f32[256,256]{1,0:T(8,128)S(1)} %get-tuple-element.129, bf16[128,256]{1,0:T(8,128)(2,1)S(1)} %get-tuple-element.130, bf16[16,4,512]{2,1,0:T(4,128)(2,1)S(1)} %dynamic-slice_bitcast_fusion.2), kind=kOutput, calls=%fused_computation.2.clone.1 | convolution fusion | flops 279967744 | bytes 532480 | tf_op jit(solution)/shard_map/while/body/eval_jaxpr/vmap()/dot_general | solution.py:48
  109.1 0.7 copy.12
  (20 shorter events, 0.4 us)
Async XLA Ops:
  0.0 1.2 %copy-start.1 = (bf16[2,4,28672]{2,1,0:T(4,128)(2,1)S(1)}, bf16[2,4,28672]{2,1,0:T(4,128)(2,1)}, u32[]{:S(2)}) copy-start(bf16[2,4,28672]{2,1,0:T(4,128)(2,1)} %param.15) | copy-start | bytes 1376260
  1.3 0.9 copy-start.2
  1.3 0.9 copy-start.3
  1.3 1.0 copy-start.4
  2.5 1.6 %copy-start = (bf16[4,32,8192]{2,1,0:T(8,128)(2,1)S(1)}, bf16[4,32,8192]{2,1,0:T(8,128)(2,1)}, u32[]{:S(2)}) copy-start(bf16[4,32,8192]{2,1,0:T(8,128)(2,1)} %param.13) | copy-start | bytes 6291460
  4.0 97.0 %copy-start.5 = (s32[4,32]{1,0:T(4,128)S(1)}, s32[4,32]{1,0:T(4,128)}, u32[]{:S(2)}) copy-start(s32[4,32]{1,0:T(4,128)} %param.14) | copy-start | bytes 1540
  101.2 1.0 copy-start.6

commit v2 on v1

--- a/solution.py
+++ b/solution.py
@@ -9,7 +9,50 @@
 
 AXES = ("layer", "tok", "qry")
 CHIPS = (4, 2, 2)
-KINDS = ("zxy",) * 5 + ("yzx",) * 3 + ("xyz",)
+EARLY = 3
+KINDS = (
+    "zyx",
+    "zxy",
+    "zxy",
+    "xyz",
+    "yzx",
+    "zxy",
+    "zyx",
+    "xyz",
+    "zyx",
+    "zyx",
+    "xzy",
+    "zxy",
+    "yxz",
+    "yxz",
+    "zyx",
+    "zxy",
+    "zxy",
+    "zyx",
+)
+ORDER = (
+    (0, -1, 0), (1, -1, 0), (2, -1, 0), (0, 0, 1), (1, 0, 1), (2, 0, 1),
+    (0, 0, 2), (3, -1, 0), (4, -1, 0), (1, 0, 2), (5, -1, 0), (2, 0, 2),
+    (3, 0, 1), (6, -1, 0), (7, -1, 0), (0, 0, 3), (1, 0, 3), (5, 0, 1),
+    (2, 0, 3), (4, 0, 1), (6, 0, 1), (5, 0, 2), (3, 1, 1), (6, 0, 2),
+    (8, -1, 0), (1, 1, 1), (5, 0, 3), (0, 1, 1), (7, 0, 1), (4, 1, 1),
+    (6, 0, 3), (2, 1, 1), (9, -1, 0), (10, -1, 0), (3, 2, 1), (8, 0, 1),
+    (4, 1, 2), (1, 2, 1), (1, 9, 0), (4, 1, 3), (11, -1, 0), (9, 0, 1),
+    (5, 1, 1), (6, 1, 1), (0, 2, 1), (0, 9, 0), (3, 2, 2), (8, 0, 2),
+    (7, 1, 1), (3, 2, 3), (3, 9, 0), (2, 2, 1), (2, 9, 0), (10, 0, 1),
+    (8, 0, 3), (11, 0, 1), (4, 2, 1), (4, 9, 0), (12, -1, 0), (9, 0, 2),
+    (9, 0, 3), (11, 0, 2), (11, 0, 3), (13, -1, 0), (7, 2, 1), (5, 2, 1),
+    (6, 2, 1), (5, 9, 0), (6, 9, 0), (14, -1, 0), (10, 1, 1), (8, 1, 1),
+    (15, -1, 0), (16, -1, 0), (11, 1, 1), (12, 0, 1), (7, 2, 2), (9, 1, 1),
+    (13, 0, 1), (17, -1, 0), (7, 2, 3), (7, 9, 0), (10, 1, 2), (8, 2, 1),
+    (8, 9, 0), (14, 0, 1), (10, 1, 3), (14, 0, 2), (15, 0, 1), (16, 0, 1),
+    (14, 0, 3), (15, 0, 2), (12, 1, 1), (16, 0, 2), (17, 0, 1), (9, 2, 1),
+    (11, 2, 1), (9, 9, 0), (11, 9, 0), (15, 0, 3), (16, 0, 3), (10, 2, 1),
+    (13, 1, 1), (10, 9, 0), (17, 0, 2), (17, 0, 3), (14, 1, 1), (15, 1, 1),
+    (12, 2, 1), (16, 1, 1), (17, 1, 1), (13, 2, 1), (12, 2, 2), (14, 2, 1),
+    (15, 2, 1), (14, 9, 0), (15, 9, 0), (12, 2, 3), (12, 9, 0), (13, 2, 2),
+    (16, 2, 1), (17, 2, 1), (16, 9, 0), (17, 9, 0), (13, 2, 3), (13, 9, 0),
+)
 
 
 def pick_positions(values, token_index):
@@ -100,12 +143,17 @@
 
 
 def rotate_kernel(
-    stack_ref,
+    out_ref,
+    in_ref,
+    own_corr_ref,
+    query_grads_ref,
+    query_acts_ref,
     grads_ref,
     acts_ref,
     rot_ref,
     query_ref,
     corr_ref,
+    stack_ref,
     basis,
     rows,
     partner,
@@ -185,10 +233,41 @@
         return carry
 
     lax.fori_loop(1, count, greet, 0)
+
+    def pack(half, at, own, query, source, width):
+        tops = own[:, pl.ds(source, width)].astype(jnp.float32)
+        if query is None:
+            ends = [jnp.zeros((8, width), jnp.float32)]
+        else:
+            ends = [
+                query[q, :, pl.ds(source, width)].astype(jnp.float32)
+                for q in range(query.shape[0])
+            ]
+        stack_ref[half, :, pl.ds(at, width)] = jnp.concatenate([tops, *ends], axis=0).astype(
+            jnp.bfloat16
+        )
+
+    for half in range(2):
+        for at in range(0, half_out, chunk):
+            pack(half, at, out_ref, query_grads_ref, half * half_out + at, chunk)
+        for at in range(0, half_in, chunk):
+            pack(half, half_out + at, in_ref, query_acts_ref, half * half_in + at, chunk)
+        pack(half, half_out + half_in, own_corr_ref, None, 0, eigen)
     pl.semaphore_wait(barrier, count - 1)
 
-    stack_copy = remote(stack_ref.at[1 - core], partner, pair_send.at[0], pair_recv.at[0], sibling)
-    stack_copy.start()
+    early = EARLY * chunk
+    stack_copies = [
+        remote(
+            stack_ref.at[1 - core, :, cols],
+            partner.at[:, cols],
+            pair_send.at[slot],
+            pair_recv.at[slot],
+            sibling,
+        )
+        for slot, cols in ((0, pl.ds(0, early)), (5, pl.ds(early, partner.shape[1] - early)))
+    ]
+    for copy in stack_copies:
+        copy.start()
     row_copies = [
         remote(
             grads_ref.at[:, pl.ds((1 - core) * half_out, half_out)],
@@ -208,7 +287,6 @@
     for copy in row_copies:
         copy.start()
     acc[...] = jnp.zeros_like(acc)
-    stack_copy.wait_recv()
 
     def build(j):
         cols = span(j)
@@ -223,44 +301,26 @@
             [first[8:], second[8:]], axis=0
         ).astype(jnp.bfloat16)
 
-    def z_block(j, source):
-        cols = span(j)
-        if KINDS[j] == "zxy":
-            return basis.at[y, x, source, :, cols]
-        if KINDS[j] == "yzx":
-            return basis.at[:, x, source, :, cols]
-        return basis.at[:, :, source, :, cols]
-
-    def x_block(j, at_x):
-        cols = span(j)
-        if KINDS[j] == "zxy":
-            return basis.at[y, at_x, :, :, cols]
-        if KINDS[j] == "yzx":
-            return basis.at[:, at_x, :, :, cols]
-        return basis.at[y, at_x, z, :, cols]
-
-    def y_block(j, at_y):
-        cols = span(j)
-        if KINDS[j] == "zxy":
-            return basis.at[at_y, :, :, :, cols]
-        if KINDS[j] == "yzx":
-            return basis.at[at_y, x, z, :, cols]
-        return basis.at[at_y, :, z, :, cols]
+    def block(j, axis, at):
+        before = KINDS[j][: KINDS[j].index(axis)]
+        place = {"y": y, "x": x, "z": z, axis: at}
+        index = [slice(None) if a in before else place[a] for a in "yxz"]
+        return basis.at[(*index, slice(None), span(j))]
 
     def up_copy(j, source):
-        ref = z_block(j, source)
+        ref = block(j, "z", source)
         return remote(ref, ref, up_send.at[j, source], z_recv.at[j, source], me + 8)
 
     def down_copy(j, source):
-        ref = z_block(j, source)
+        ref = block(j, "z", source)
         return remote(ref, ref, down_send.at[j, source], z_recv.at[j, source], me - 8)
 
     def x_copy(j, at_x):
-        ref = x_block(j, at_x)
+        ref = block(j, "x", at_x)
         return remote(ref, ref, side_send.at[0, j], side_recv.at[0, j], x_peer)
 
     def y_copy(j, at_y):
-        ref = y_block(j, at_y)
+        ref = block(j, "y", at_y)
         return remote(ref, ref, side_send.at[1, j], side_recv.at[1, j], y_peer)
 
     def z_start(j):
@@ -323,80 +383,30 @@
         )
 
     last = len(KINDS) - 1
-    for j in (0, 5, 8, 1, 6, 2, 7, 3, 4):
-        build(j)
-        {"z": z_start, "x": x_start, "y": y_start}[KINDS[j][0]](j)
-    for j in (0, 1, 2):
-        z_step(j, 1)
-    x_wait(8)
-    y_start(8)
-    for j in (0, 1, 2):
-        z_step(j, 2)
-    for j in (0, 1, 2):
-        z_step(j, 3)
-        x_start(j)
-    y_wait(5)
-    z_start(5)
-    z_step(3, 1)
-    z_step(4, 1)
-    x_wait(0)
-    y_start(0)
-    z_step(5, 1)
-    z_step(3, 2)
-    z_step(4, 2)
-    y_wait(6)
-    z_start(6)
-    x_wait(1)
-    y_start(1)
-    z_step(5, 2)
-    z_step(3, 3)
-    x_start(3)
-    x_wait(2)
-    y_start(2)
-    z_step(5, 3)
-    x_start(5)
-    z_step(4, 3)
-    x_start(4)
-    z_step(6, 1)
-    y_wait(7)
-    z_start(7)
-    for copy in own_copies:
-        copy.wait()
-    for copy in row_copies:
-        copy.wait_recv()
-    y_wait(0)
-    compute(0)
-    z_step(6, 2)
-    x_wait(3)
-    y_start(3)
-    z_step(6, 3)
-    x_start(6)
-    y_wait(8)
-    z_start(8)
-    z_step(7, 1)
-    x_wait(4)
-    y_start(4)
-    y_wait(1)
-    compute(1)
-    z_step(7, 2)
-    x_wait(5)
-    compute(5)
-    z_step(8, 1)
-    z_step(7, 3)
-    x_start(7)
-    y_wait(2)
-    compute(2)
-    z_step(8, 2)
-    y_wait(3)
-    compute(3)
-    x_wait(6)
-    compute(6)
-    z_step(8, 3)
-    compute(8)
-    y_wait(4)
-    compute(4)
-    x_wait(7)
-    compute(7)
+    starts = {"z": z_start, "x": x_start, "y": y_start}
+    rows_here = False
+    for j, place, step in ORDER:
+        if place < 0:
+            if j in (0, EARLY):
+                stack_copies[j // EARLY].wait_recv()
+            build(j)
+            starts[KINDS[j][0]](j)
+        elif place < len(KINDS[j]):
+            axis = KINDS[j][place]
+            if axis == "z":
+                z_step(j, step)
+            else:
+                {"x": x_wait, "y": y_wait}[axis](j)
+            if place + 1 < len(KINDS[j]) and (axis != "z" or step == nz - 1):
+                starts[KINDS[j][place + 1]](j)
+        else:
+            if not rows_here:
+                rows_here = True
+                for copy in own_copies:
+                    copy.wait()
+                for copy in row_copies:
+                    copy.wait_recv()
+            compute(j)
 
     qpart_out[...] = acc[1 - core, pl.ds(2 * train, 16), :]
     qpart_copy = remote(qpart_out, qpart_in, pair_send.at[3], pair_recv.at[3], sibling)
@@ -420,16 +430,7 @@
     part_copy.wait_recv()
     rot_ref[...] = (acc[:, pl.ds(0, train), :] + part_in[...]).astype(jnp.bfloat16)
 
-    def wait_query(s, carry):
-        source = lax.rem(me + s, count)
-        query_copy(source, source).wait_recv()
-        return carry
-
-    lax.fori_loop(1, count, wait_query, 0)
-    query_ref[...] = queries[...].reshape(query_ref.shape)
-
-    stack_copy.wait_send()
-    for copy in row_copies:
+    for copy in stack_copies + row_copies:
         copy.wait_send()
     qpart_copy.wait_send()
     part_copy.wait_send()
@@ -446,6 +447,14 @@
             def _():
                 down_copy(j, z + s).wait_send()
 
+    def wait_query(s, carry):
+        source = lax.rem(me + s, count)
+        query_copy(source, source).wait_recv()
+        return carry
+
+    lax.fori_loop(1, count, wait_query, 0)
+    query_ref[...] = queries[...].reshape(query_ref.shape)
+
     def finish_query(s, carry):
         query_copy(me, lax.rem(me + s, count)).wait_send()
         return carry
@@ -453,15 +462,16 @@
     lax.fori_loop(1, count, finish_query, 0)
 
 
-def rotate_all(stack, grads, acts, eigen):
+def rotate_all(out_basis, in_basis, corrections, query_grads, query_acts, grads, acts):
     train, wide = grads.shape
-    total = stack.shape[2]
+    eigen = corrections.shape[1]
+    total = (wide + acts.shape[1]) // 2 + eigen
     nz, ny, nx = CHIPS
     chips = nz * ny * nx
     n = len(KINDS)
     dma = pltpu.SemaphoreType.DMA
     vmem = pl.BlockSpec(memory_space=pltpu.VMEM)
-    hbm = pl.BlockSpec(memory_space=pl.ANY)
+    hbm = pl.BlockSpec(memory_space=pltpu.HBM)
     return pl.pallas_call(
         rotate_kernel,
         out_shape=(
@@ -469,9 +479,10 @@
             jax.ShapeDtypeStruct((2, chips * 16, eigen), jnp.bfloat16),
             jax.ShapeDtypeStruct((eigen, eigen), jnp.bfloat16),
         ),
-        in_specs=[vmem, hbm, hbm],
+        in_specs=[vmem] * 5 + [hbm] * 2,
         out_specs=(vmem, vmem, vmem),
         scratch_shapes=[
+            pltpu.VMEM((2, 16, total), jnp.bfloat16),
             pltpu.VMEM((ny, nx, nz, 16, total), jnp.bfloat16),
             pltpu.VMEM((2 * train + 16, total), jnp.bfloat16),
             pltpu.VMEM((16, total), jnp.bfloat16),
@@ -482,8 +493,8 @@
             pltpu.VMEM((16, eigen), jnp.float32),
             pltpu.VMEM((2, chips, 16, eigen), jnp.bfloat16),
             dma((2,)),
-            dma((5,)),
-            dma((5,)),
+            dma((6,)),
+            dma((6,)),
             dma((n, nz)),
             dma((n, nz)),
             dma((n, nz)),
@@ -493,12 +504,12 @@
             dma((2 * chips,)),
         ],
         compiler_params=pltpu.CompilerParams(
-            collective_id=0, has_side_effects=True, vmem_limit_bytes=44 * 1024 * 1024
+            collective_id=0, has_side_effects=True, vmem_limit_bytes=53 * 1024 * 1024
         ),
         cost_estimate=pl.CostEstimate(
             flops=4 * train * total * eigen, bytes_accessed=4 * train * wide, transcendentals=0
         ),
-    )(stack, grads, acts)
+    )(out_basis, in_basis, corrections, query_grads, query_acts, grads, acts)
 
 
 def local_fused(
@@ -516,31 +527,16 @@
     eigen = corrections.shape[1]
     seq_count, sel_count = token_index.shape
     length = train_grads.shape[1]
-    query_count, query_len = query_grads.shape[:2]
-    rows_q = query_count * query_len
+    query_len = query_grads.shape[1]
     wide_out, wide_in = out_basis.shape[1], in_basis.shape[1]
-    out_rows = jnp.concatenate([out_basis, query_grads.reshape(rows_q, wide_out)], axis=0)
-    in_rows = jnp.concatenate([in_basis, query_acts.reshape(rows_q, wide_in)], axis=0)
-    corr_rows = jnp.concatenate([corrections, jnp.zeros((rows_q, eigen), corrections.dtype)], axis=0)
-    stack = jnp.stack(
-        [
-            jnp.concatenate(
-                [
-                    out_rows[:, h * (wide_out // 2) : (h + 1) * (wide_out // 2)],
-                    in_rows[:, h * (wide_in // 2) : (h + 1) * (wide_in // 2)],
-                    corr_rows,
-                ],
-                axis=1,
-            )
-            for h in range(2)
-        ],
-        axis=0,
-    )
     rot, queries, corr = rotate_all(
-        stack,
+        out_basis,
+        in_basis,
+        corrections,
+        query_grads,
+        query_acts,
         train_grads.reshape(-1, wide_out),
         train_acts.reshape(-1, wide_in),
-        eigen,
     )
     one_hot = (token_index[:, :, None] == jnp.arange(length, dtype=token_index.dtype)).astype(
         jnp.bfloat16

time: 111 us -> 107 us (0.964)
  Pallas kernels: 96.9 us -> 95.3 us
  local copies, waits for them, and re-layouts: 4.81 us -> 3.56 us
    pallas_call x1, Pallas kernels: 96.9 us -> 95.3 us  [rotate_all(): pl.pallas_call(rotate_kernel, out_shape=(jax.ShapeDtypeStruct((2, train,...]
    unnamed x16 -> x10, local copies, waits for them, and re-layouts: 3.48 us -> 2.5 us
where the time goes in v2:
time: 107 us
  Pallas kernels  95.3 us (89%)
  matrix products  5.46 us (5%)
  local copies, waits for them, and re-layouts  3.56 us (3%)
  other arithmetic  1.41 us (1%)
    pallas_call x1, Pallas kernels, rotate_all(): pl.pallas_call(rotate_kernel, out_shape=(jax.ShapeDtypeStruct((2, train,...  95.3 us
    dot_general x4, matrix products, score_query(): lax.dot_general(token_in, precond, (((1,), (1,)), ((), ())), preferred_el...  5.24 us
    unnamed x10, local copies, waits for them, and re-layouts  2.5 us

profile of v2, /device:TPU:0, one launch (start us, length us, event | category | flops | bytes accessed | tf_op | source)
XLA Modules:
  0.0 106.7 jit_solution(480622052977464694)
XLA Ops:
  0.0 0.0 copy-start
  0.0 0.9 copy-done
  0.9 0.0 copy-start.1
  0.9 0.9 copy-done.1
  1.8 0.0 copy-start.2
  1.8 0.7 copy-done.2
  2.5 0.0 copy-start.3
  2.5 95.3 %shard_map.100 = (bf16[2,128,256]{2,1,0:T(8,128)(2,1)S(1)}, bf16[2,256,256]{2,1,0:T(8,128)(2,1)S(1)}, bf16[256,256]{1,0:T(8,128)(2,1)S(1)}) custom-call(bf16[8,28672]{1,0:T(8,128)(2,1)} %out_ref.1, bf16[8,8192]{1,0:T(8,128)(2,1)S(1)} %copy-done, bf16[8,256]{1,0:T(8,128)(2,1)S(1)} %copy-done.2, bf16[2,4,28672]{2,1,0:T(4,128)(2,1)} %query_grads_ref.1, ...), custom_call_target="tpu_custom_call" | custom-call | flops 2449473536 | bytes 14680064 | tf_op jit(solution)/shard_map/pallas_call | solution.py:475
  97.8 0.0 copy-start.4
  97.9 0.0 copy-done.3
  97.9 0.2 convolution_convert_fusion
  98.2 0.1 copy.11
  98.4 0.1 pad_maximum_fusion
  99.1 0.0 copy-done.4
  99.1 0.6 fusion.11
  99.8 0.6 convert_add_fusion
  100.4 5.5 %while.10 = (s32[]{:T(128)}, f32[4,16,128]{2,1,0:T(8,128)S(1)}, f32[128,256]{0,1:T(8,128)S(1)}, bf16[4,16,4,512]{3,2,1,0:T(4,128)(2,1)S(1)}, f32[256,256]{1,0:T(...) while((s32[]{:T(128)}, f32[4,16,128]{2,1,0:T(8,128)S(1)}, f32[128,256]{0,1:T(8,128)S(1)}, ...), condition=%wide.region_3.4_spmd, body=%wide.region_1.3_spmd.sunk | while | flops 279969792 | bytes 680021 | solution.py:97
  100.5 1.3 %fusion.23 = f32[16,128]{1,0:T(8,128)S(1)} fusion(f32[128,256]{0,1:T(8,128)S(1)} %get-tuple-element.121, f32[256,256]{1,0:T(8,128)S(1)} %get-tuple-element.123, bf16[128,256]{1,0:T(8,128)(2,1)S(1)} %get-tuple-element.124, bf16[16,4,512]{2,1,0:T(4,128)(2,1)S(1)} %dynamic-slice_bitcast_fusion.2), kind=kOutput, calls=%fused_computation.2.clone.1 | convolution fusion | flops 279967744 | bytes 532480 | tf_op jit(solution)/shard_map/while/body/eval_jaxpr/vmap()/dot_general | solution.py:91
  101.8 1.3 %fusion.23 = f32[16,128]{1,0:T(8,128)S(1)} fusion(f32[128,256]{0,1:T(8,128)S(1)} %get-tuple-element.121, f32[256,256]{1,0:T(8,128)S(1)} %get-tuple-element.123, bf16[128,256]{1,0:T(8,128)(2,1)S(1)} %get-tuple-element.124, bf16[16,4,512]{2,1,0:T(4,128)(2,1)S(1)} %dynamic-slice_bitcast_fusion.2), kind=kOutput, calls=%fused_computation.2.clone.1 | convolution fusion | flops 279967744 | bytes 532480 | tf_op jit(solution)/shard_map/while/body/eval_jaxpr/vmap()/dot_general | solution.py:91
  103.2 1.3 %fusion.23 = f32[16,128]{1,0:T(8,128)S(1)} fusion(f32[128,256]{0,1:T(8,128)S(1)} %get-tuple-element.121, f32[256,256]{1,0:T(8,128)S(1)} %get-tuple-element.123, bf16[128,256]{1,0:T(8,128)(2,1)S(1)} %get-tuple-element.124, bf16[16,4,512]{2,1,0:T(4,128)(2,1)S(1)} %dynamic-slice_bitcast_fusion.2), kind=kOutput, calls=%fused_computation.2.clone.1 | convolution fusion | flops 279967744 | bytes 532480 | tf_op jit(solution)/shard_map/while/body/eval_jaxpr/vmap()/dot_general | solution.py:91
  104.6 1.3 %fusion.23 = f32[16,128]{1,0:T(8,128)S(1)} fusion(f32[128,256]{0,1:T(8,128)S(1)} %get-tuple-element.121, f32[256,256]{1,0:T(8,128)S(1)} %get-tuple-element.123, bf16[128,256]{1,0:T(8,128)(2,1)S(1)} %get-tuple-element.124, bf16[16,4,512]{2,1,0:T(4,128)(2,1)S(1)} %dynamic-slice_bitcast_fusion.2), kind=kOutput, calls=%fused_computation.2.clone.1 | convolution fusion | flops 279967744 | bytes 532480 | tf_op jit(solution)/shard_map/while/body/eval_jaxpr/vmap()/dot_general | solution.py:91
  106.0 0.7 copy.12
  (15 shorter events, 0.3 us)
Async XLA Ops:
  0.0 0.9 copy-start
  0.9 0.9 copy-start.1
  1.8 0.7 copy-start.2
  2.5 95.4 %copy-start.3 = (s32[4,32]{1,0:T(4,128)S(1)}, s32[4,32]{1,0:T(4,128)}, u32[]{:S(2)}) copy-start(s32[4,32]{1,0:T(4,128)} %param.14) | copy-start | bytes 1540
  97.8 1.3 %copy-start.4 = (f32[80]{0:T(128)S(1)}, f32[80]{0:T(128)}, u32[]{:S(2)}) copy-start(f32[80]{0:T(128)} %param.20) | copy-start | bytes 964

commit v3 on v2

--- a/solution.py
+++ b/solution.py
@@ -181,7 +181,7 @@
     y = lax.rem(me // 4, 2)
     z = me // 8
     nz = CHIPS[0]
-    count = 2 * nz * CHIPS[1] * CHIPS[2]
+    chips = nz * CHIPS[1] * CHIPS[2]
     sibling = me + 1 - 2 * core
     x_peer = me + 2 - 4 * x
     y_peer = me + 4 - 8 * y
@@ -221,18 +221,24 @@
     for copy in own_copies:
         copy.start()
 
+    def peer(s):
+        return 2 * lax.rem(chip + s, chips) + core
+
     barrier = pltpu.get_barrier_semaphore()
+    pl.semaphore_signal(
+        barrier, inc=1, device_id=(0, sibling, 0), device_id_type=pl.DeviceIdType.MESH
+    )
 
     def greet(s, carry):
         pl.semaphore_signal(
             barrier,
             inc=1,
-            device_id=(0, lax.rem(me + s, count), 0),
+            device_id=(0, peer(s), 0),
             device_id_type=pl.DeviceIdType.MESH,
         )
         return carry
 
-    lax.fori_loop(1, count, greet, 0)
+    lax.fori_loop(1, chips, greet, 0)
 
     def pack(half, at, own, query, source, width):
         tops = own[:, pl.ds(source, width)].astype(jnp.float32)
@@ -253,7 +259,7 @@
         for at in range(0, half_in, chunk):
             pack(half, half_out + at, in_ref, query_acts_ref, half * half_in + at, chunk)
         pack(half, half_out + half_in, own_corr_ref, None, 0, eigen)
-    pl.semaphore_wait(barrier, count - 1)
+    pl.semaphore_wait(barrier, chips)
 
     early = EARLY * chunk
     stack_copies = [
@@ -422,10 +428,10 @@
         return remote(ref, ref, query_send.at[target], query_recv.at[source], target)
 
     def send_query(s, carry):
-        query_copy(me, lax.rem(me + s, count)).start()
+        query_copy(me, peer(s)).start()
         return carry
 
-    lax.fori_loop(1, count, send_query, 0)
+    lax.fori_loop(1, chips, send_query, 0)
     corr_ref[...] = natural(pl.ds(half_out + half_in, eigen))
     part_copy.wait_recv()
     rot_ref[...] = (acc[:, pl.ds(0, train), :] + part_in[...]).astype(jnp.bfloat16)
@@ -448,18 +454,24 @@
                 down_copy(j, z + s).wait_send()
 
     def wait_query(s, carry):
-        source = lax.rem(me + s, count)
+        source = peer(s)
         query_copy(source, source).wait_recv()
         return carry
 
-    lax.fori_loop(1, count, wait_query, 0)
+    lax.fori_loop(1, chips, wait_query, 0)
+    mine = queries.at[core]
+    share = remote(mine, mine, pair_send.at[6], pair_recv.at[6], sibling)
+    share.start()
+
+    def finish_query(s, carry):
+        query_copy(me, peer(s)).wait_send()
+        return carry
+
+    lax.fori_loop(1, chips, finish_query, 0)
+    theirs = queries.at[1 - core]
+    remote(theirs, theirs, pair_send.at[6], pair_recv.at[6], sibling).wait_recv()
     query_ref[...] = queries[...].reshape(query_ref.shape)
-
-    def finish_query(s, carry):
-        query_copy(me, lax.rem(me + s, count)).wait_send()
-        return carry
-
-    lax.fori_loop(1, count, finish_query, 0)
+    share.wait_send()
 
 
 def rotate_all(out_basis, in_basis, corrections, query_grads, query_acts, grads, acts):
@@ -493,8 +505,8 @@
             pltpu.VMEM((16, eigen), jnp.float32),
             pltpu.VMEM((2, chips, 16, eigen), jnp.bfloat16),
             dma((2,)),
-            dma((6,)),
-            dma((6,)),
+            dma((7,)),
+            dma((7,)),
             dma((n, nz)),
             dma((n, nz)),
             dma((n, nz)),

time: 107 us -> 109 us (1.019)
  Pallas kernels: 95.3 us -> 97.1 us
    pallas_call x1, Pallas kernels: 95.3 us -> 97.1 us  [rotate_all(): pl.pallas_call(rotate_kernel, out_shape=(jax.ShapeDtypeStruct((2, train,...]
where the time goes in v3:
time: 109 us; the launch traced here: 108 us
  Pallas kernels  97.1 us (89%)
  matrix products  5.46 us (5%)
  local copies, waits for them, and re-layouts  3.56 us (3%)
  other arithmetic  1.41 us (1%)
    pallas_call x1, Pallas kernels, rotate_all(): pl.pallas_call(rotate_kernel, out_shape=(jax.ShapeDtypeStruct((2, train,...  97.1 us
    dot_general x4, matrix products, score_query(): lax.dot_general(token_in, precond, (((1,), (1,)), ((), ())), preferred_el...  5.23 us
    unnamed x10, local copies, waits for them, and re-layouts  2.5 us

profile of v3, /device:TPU:0, one launch (start us, length us, event | category | flops | bytes accessed | tf_op | source)
XLA Modules:
  0.0 108.4 jit_solution(17345890305884321902)
XLA Ops:
  0.0 0.0 copy-start
  0.0 0.9 copy-done
  0.9 0.0 copy-start.1
  0.9 0.9 copy-done.1
  1.8 0.0 copy-start.2
  1.8 0.7 copy-done.2
  2.5 0.0 copy-start.3
  2.5 97.1 %shard_map.100 = (bf16[2,128,256]{2,1,0:T(8,128)(2,1)S(1)}, bf16[2,256,256]{2,1,0:T(8,128)(2,1)S(1)}, bf16[256,256]{1,0:T(8,128)(2,1)S(1)}) custom-call(bf16[8,28672]{1,0:T(8,128)(2,1)} %out_ref.1, bf16[8,8192]{1,0:T(8,128)(2,1)S(1)} %copy-done, bf16[8,256]{1,0:T(8,128)(2,1)S(1)} %copy-done.2, bf16[2,4,28672]{2,1,0:T(4,128)(2,1)} %query_grads_ref.1, ...), custom_call_target="tpu_custom_call" | custom-call | flops 2449473536 | bytes 14680064 | tf_op jit(solution)/shard_map/pallas_call | solution.py:487
  99.6 0.0 copy-start.4
  99.6 0.0 copy-done.3
  99.6 0.2 convolution_convert_fusion
  99.9 0.1 copy.11
  100.1 0.1 pad_maximum_fusion
  100.9 0.0 copy-done.4
  100.9 0.6 fusion.11
  101.5 0.6 convert_add_fusion
  102.2 5.5 %while.10 = (s32[]{:T(128)}, f32[4,16,128]{2,1,0:T(8,128)S(1)}, f32[128,256]{0,1:T(8,128)S(1)}, bf16[4,16,4,512]{3,2,1,0:T(4,128)(2,1)S(1)}, f32[256,256]{1,0:T(...) while((s32[]{:T(128)}, f32[4,16,128]{2,1,0:T(8,128)S(1)}, f32[128,256]{0,1:T(8,128)S(1)}, ...), condition=%wide.region_3.4_spmd, body=%wide.region_1.3_spmd.sunk | while | flops 279969792 | bytes 680021 | solution.py:97
  102.2 1.3 %fusion.23 = f32[16,128]{1,0:T(8,128)S(1)} fusion(f32[128,256]{0,1:T(8,128)S(1)} %get-tuple-element.121, f32[256,256]{1,0:T(8,128)S(1)} %get-tuple-element.123, bf16[128,256]{1,0:T(8,128)(2,1)S(1)} %get-tuple-element.124, bf16[16,4,512]{2,1,0:T(4,128)(2,1)S(1)} %dynamic-slice_bitcast_fusion.2), kind=kOutput, calls=%fused_computation.2.clone.1 | convolution fusion | flops 279967744 | bytes 532480 | tf_op jit(solution)/shard_map/while/body/eval_jaxpr/vmap()/dot_general | solution.py:91
  103.6 1.3 %fusion.23 = f32[16,128]{1,0:T(8,128)S(1)} fusion(f32[128,256]{0,1:T(8,128)S(1)} %get-tuple-element.121, f32[256,256]{1,0:T(8,128)S(1)} %get-tuple-element.123, bf16[128,256]{1,0:T(8,128)(2,1)S(1)} %get-tuple-element.124, bf16[16,4,512]{2,1,0:T(4,128)(2,1)S(1)} %dynamic-slice_bitcast_fusion.2), kind=kOutput, calls=%fused_computation.2.clone.1 | convolution fusion | flops 279967744 | bytes 532480 | tf_op jit(solution)/shard_map/while/body/eval_jaxpr/vmap()/dot_general | solution.py:91
  105.0 1.3 %fusion.23 = f32[16,128]{1,0:T(8,128)S(1)} fusion(f32[128,256]{0,1:T(8,128)S(1)} %get-tuple-element.121, f32[256,256]{1,0:T(8,128)S(1)} %get-tuple-element.123, bf16[128,256]{1,0:T(8,128)(2,1)S(1)} %get-tuple-element.124, bf16[16,4,512]{2,1,0:T(4,128)(2,1)S(1)} %dynamic-slice_bitcast_fusion.2), kind=kOutput, calls=%fused_computation.2.clone.1 | convolution fusion | flops 279967744 | bytes 532480 | tf_op jit(solution)/shard_map/while/body/eval_jaxpr/vmap()/dot_general | solution.py:91
  106.4 1.3 %fusion.23 = f32[16,128]{1,0:T(8,128)S(1)} fusion(f32[128,256]{0,1:T(8,128)S(1)} %get-tuple-element.121, f32[256,256]{1,0:T(8,128)S(1)} %get-tuple-element.123, bf16[128,256]{1,0:T(8,128)(2,1)S(1)} %get-tuple-element.124, bf16[16,4,512]{2,1,0:T(4,128)(2,1)S(1)} %dynamic-slice_bitcast_fusion.2), kind=kOutput, calls=%fused_computation.2.clone.1 | convolution fusion | flops 279967744 | bytes 532480 | tf_op jit(solution)/shard_map/while/body/eval_jaxpr/vmap()/dot_general | solution.py:91
  107.7 0.7 copy.12
  (15 shorter events, 0.3 us)
Async XLA Ops:
  0.0 0.9 copy-start
  0.9 0.9 copy-start.1
  1.8 0.7 copy-start.2
  2.5 97.1 %copy-start.3 = (s32[4,32]{1,0:T(4,128)S(1)}, s32[4,32]{1,0:T(4,128)}, u32[]{:S(2)}) copy-start(s32[4,32]{1,0:T(4,128)} %param.14) | copy-start | bytes 1540
  99.6 1.3 %copy-start.4 = (f32[80]{0:T(128)S(1)}, f32[80]{0:T(128)}, u32[]{:S(2)}) copy-start(f32[80]{0:T(128)} %param.20) | copy-start | bytes 964
